TPU v7x, 32 devices: a whole 2x2x4 slice. The times are simulated.
32 devices in a mesh: groups: 2 (over y), ctx: 4 (over z), dp: 2 (over x), mp: 2 (over core).
Axes of the slice: x: 2, y: 2, z: 4, core: 2. Of those that a mesh axis runs over, the one named last changes fastest.
Arguments:
- head_inputs: bfloat16 [3, 4, 1024, 1536], P(None, ('groups', 'dp'), 'ctx', 'mp'), parts along dimension 1, may hold values from -0.29882812 to 0.29882812
- write_read: bfloat16 [3, 4, 1024, 128], P(None, ('groups', 'dp'), 'ctx'), parts along dimension 1, may hold values from -0.26953125 to 0.26953125
- decay_steps: int32 [3, 4, 12, 1024], P(None, ('groups', 'dp'), 'mp', 'ctx'), parts along dimension 1, may hold values from 0 to 512
- scan_orders: int32 [2, 4, 1024], P(None, ('groups', 'dp'), 'ctx'), parts along dimension 1, may hold values from 0 to 1023, as said below
- cotangent: bfloat16 [4, 1024, 768], P(('groups', 'dp'), 'ctx'), parts along dimension 0, may hold values from -0.59765625 to 0.59765625
- out_weight: bfloat16 [3, 768, 1536], P(None, 'ctx', 'mp'), may hold values from -0.4375 to 0.4375
Outputs:
- grad_inputs: bfloat16 [3, 4, 1024, 1536], P(None, ('groups', 'dp'), 'ctx', 'mp'), parts along dimension 1
- grad_write_read: bfloat16 [3, 4, 1024, 128], P(None, ('groups', 'dp'), 'ctx'), parts along dimension 1
- grad_weight: bfloat16 [6, 768, 1536], P('groups', 'ctx', 'mp'), parts along dimension 0
There are 2 independent parts, one for each index of `groups`. A program takes and returns all parts, laid end to end along the dimension named above; an argument that names none is the same for every part. Nothing has to cross between parts.
Inputs may be any that keep to these rules, and one draw needn't show every extreme that they name: `scan_orders`: for every volume and each of the two orders, position d * 256 + q * 64 + m (0 <= m < 64) holds a patch of index q * 256 + d * 64 + m' with 0 <= m' < 64; every patch stands at exactly one position.
All inputs are finite; a program needn't handle non-finite values.
Results may differ from a plain program's by a relative error of at most 0.005.
Values may be sent and summed in bfloat16 or wider, within the bound.
A program may use at most 128 MiB of HBM per device.

v0:
```python
import math
import jax
import jax.numpy as jnp
from jax import lax
from jax.sharding import PartitionSpec as P

P_SIZE = 128
N = 64
EXACT = lax.Precision.HIGHEST


def prefix(value, axis, join, neutral, backward):
    count, mine = (lax.axis_size(axis), lax.axis_index(axis))
    pieces = jax.tree.map(lambda part: lax.all_gather(part, axis), value)
    if backward:
        pieces = jax.tree.map(lambda part: part[::-1], pieces)
        mine = count - 1 - mine
    running = jax.tree.map(
        lambda part, zero: jnp.full_like(part, 0) + jnp.asarray(zero, part.dtype), value, neutral
    )

    def lap(position, running):
        longer = join(running, jax.tree.map(lambda part: part[position], pieces))
        return jax.tree.map(lambda new, old: jnp.where(position < mine, new, old), longer, running)

    return lax.fori_loop(0, count - 1, lap, running)


def contract(form, *operands):
    return jnp.einsum(form, *operands, precision=EXACT)


def segment_parts(log_rates, writes, readers):
    running = jnp.cumsum(log_rates, axis=-1)
    final_log = running[..., -1]
    length = log_rates.shape[-1]
    causal = jnp.arange(length)[:, None] >= jnp.arange(length)[None, :]
    differ = jnp.where(causal, running[..., :, None] - running[..., None, :], 0.0)
    decay_mat = jnp.where(causal, jnp.exp(differ), 0.0)
    scores = contract("ovin,ovjn->ovij", readers, writes)
    mixing = scores[:, :, None] * decay_mat
    return (running, final_log, decay_mat, mixing)


def segment_forward(pieces, signal, writes, readers, memory):
    running, final_log, decay_mat, mixing = pieces
    rising = jnp.exp(running)
    falling = jnp.exp(final_log[..., None] - running)
    outputs = contract("ovhij,ovjhp->ovihp", mixing, signal) + contract(
        "ovhi,ovin,ovhnp->ovihp", rising, readers, memory
    )
    memory_next = jnp.exp(final_log)[..., None, None] * memory + contract(
        "ovhj,ovjn,ovjhp->ovhnp", falling, writes, signal
    )
    return (outputs, memory_next)


def segment_backward(pieces, signal, writes, readers, upstream, memory, memory_grad):
    running, final_log, decay_mat, mixing = pieces
    rising = jnp.exp(running)
    falling = jnp.exp(final_log[..., None] - running)
    grad_signal = contract("ovhij,ovihp->ovjhp", mixing, upstream) + contract(
        "ovhj,ovjn,ovhnp->ovjhp", falling, writes, memory_grad
    )
    weighted = contract("ovihp,ovjhp->ovhij", upstream, signal) * decay_mat
    grad_writes = contract("ovhij,ovin->ovjn", weighted, readers) + contract(
        "ovhj,ovjhp,ovhnp->ovjn", falling, signal, memory_grad
    )
    grad_readers = contract("ovhij,ovjn->ovin", weighted, writes) + contract(
        "ovhi,ovihp,ovhnp->ovin", rising, upstream, memory
    )
    grad_prev = jnp.exp(final_log)[..., None, None] * memory_grad + contract(
        "ovhi,ovin,ovihp->ovhnp", rising, readers, upstream
    )
    return (grad_signal, grad_writes, grad_readers, grad_prev)


def run_segments(signal, writes, readers, log_rates, upstream, memory_in, grad_in, length):
    blocks = signal.shape[2] // length

    def cut_rows(array, number, along):
        start_row = (number * length).astype(jnp.int32)
        return lax.dynamic_slice_in_dim(array, start_row, length, along)

    def forward_turn(number, carried):
        memory, outputs, memories = carried
        sig = cut_rows(signal, number, 2)
        wri = cut_rows(writes, number, 2)
        rea = cut_rows(readers, number, 2)
        pieces = segment_parts(cut_rows(log_rates, number, 3), wri, rea)
        out_rows, memory_next = segment_forward(pieces, sig, wri, rea, memory)
        outputs = lax.dynamic_update_slice_in_dim(
            outputs, out_rows, (number * length).astype(jnp.int32), 2
        )
        memories = lax.dynamic_update_index_in_dim(memories, memory, number, 0)
        return (memory_next, outputs, memories)

    start_memories = jnp.zeros((blocks,) + memory_in.shape, memory_in.dtype)
    _, outputs, memories = lax.fori_loop(
        0, blocks, forward_turn, (memory_in, jnp.zeros_like(signal), start_memories)
    )

    def backward_turn(countdown, carried):
        memory_grad, grad_signal, grad_writes, grad_readers = carried
        number = blocks - 1 - countdown
        sig = cut_rows(signal, number, 2)
        wri = cut_rows(writes, number, 2)
        rea = cut_rows(readers, number, 2)
        pieces = segment_parts(cut_rows(log_rates, number, 3), wri, rea)
        memory = lax.dynamic_index_in_dim(memories, number, 0, keepdims=False)
        part_sig, part_wri, part_rea, grad_prev = segment_backward(
            pieces, sig, wri, rea, cut_rows(upstream, number, 2), memory, memory_grad
        )
        start_row = (number * length).astype(jnp.int32)
        grad_signal = lax.dynamic_update_slice_in_dim(grad_signal, part_sig, start_row, 2)
        grad_writes = lax.dynamic_update_slice_in_dim(grad_writes, part_wri, start_row, 2)
        grad_readers = lax.dynamic_update_slice_in_dim(grad_readers, part_rea, start_row, 2)
        return (grad_prev, grad_signal, grad_writes, grad_readers)

    _, grad_signal, grad_writes, grad_readers = lax.fori_loop(
        0,
        blocks,
        backward_turn,
        (grad_in, jnp.zeros_like(signal), jnp.zeros_like(writes), jnp.zeros_like(readers)),
    )
    return (outputs, grad_signal, grad_writes, grad_readers)


def carry_forward(earlier, later):
    return (earlier[0] + later[0], jnp.exp(later[0])[..., None, None] * earlier[1] + later[1])


def carry_backward(earlier, later):
    return (earlier[0] + later[0], later[1] + jnp.exp(later[0])[..., None, None] * earlier[1])


def shards(head_inputs, write_read, decay_steps, scan_orders, cotangent, out_weight):
    volumes, tokens, model_width = cotangent.shape
    ctx_count = lax.axis_size("ctx")
    seq_len = tokens * ctx_count
    local_heads = decay_steps.shape[2]
    inner_width = head_inputs.shape[3]
    gathered = lax.all_gather(cotangent, "ctx", axis=1, tiled=True)

    def reorder(ordering):
        return jax.vmap(lambda table_rows, row_ids: table_rows[row_ids])(gathered, ordering)

    scanned = jnp.stack([cotangent, reorder(scan_orders[0]), reorder(scan_orders[1])])
    upstream = jnp.einsum(
        "ovtd,odi->ovti",
        scanned,
        lax.all_gather(out_weight, "ctx", axis=1, tiled=True),
        preferred_element_type=jnp.float32,
    ).astype(jnp.bfloat16)
    upstream = lax.optimization_barrier(upstream)
    signal = head_inputs.astype(jnp.float32).reshape(3, volumes, tokens, local_heads, P_SIZE)
    grad_up = upstream.astype(jnp.float32).reshape(3, volumes, tokens, local_heads, P_SIZE)
    writes = write_read[..., :N].astype(jnp.float32)
    readers = write_read[..., N:].astype(jnp.float32)
    log_rates = -decay_steps.astype(jnp.float32) / seq_len
    running = jnp.cumsum(log_rates, axis=-1)
    summed_log = running[..., -1]
    end_state = contract(
        "ovht,ovtn,ovthp->ovhnp", jnp.exp(summed_log[..., None] - running), writes, signal
    )
    start_grad = contract("ovht,ovtn,ovthp->ovhnp", jnp.exp(running), readers, grad_up)
    zeros_log = jnp.zeros_like(summed_log)
    zeros_state = jnp.zeros_like(end_state)
    _, state_in = prefix(
        (summed_log, end_state), "ctx", carry_forward, (zeros_log, zeros_state), False
    )
    _, grad_out = prefix(
        (summed_log, start_grad), "ctx", carry_backward, (zeros_log, zeros_state), True
    )
    length = math.gcd(tokens, 128)
    outputs, grad_signal, grad_writes, grad_readers = run_segments(
        signal, writes, readers, log_rates, grad_up, state_in, grad_out, length
    )
    grad_wr = lax.psum(jnp.concatenate([grad_writes, grad_readers], axis=-1), "mp").astype(
        jnp.bfloat16
    )
    grad_inputs = grad_signal.reshape(3, volumes, tokens, inner_width).astype(jnp.bfloat16)
    outputs_bf = outputs.reshape(3, volumes, tokens, inner_width).astype(jnp.bfloat16)
    weight_term = jnp.einsum(
        "ovtd,ovti->odi", scanned, outputs_bf, preferred_element_type=jnp.float32
    )
    rows_sum = lax.psum_scatter(weight_term, "ctx", scatter_dimension=1, tiled=True)
    weight_grad = lax.psum(rows_sum, "dp").astype(jnp.bfloat16)
    return (grad_inputs, grad_wr, weight_grad)


def solution(mesh):
    in_specs = (
        P(None, ("groups", "dp"), "ctx", "mp"),
        P(None, ("groups", "dp"), "ctx", None),
        P(None, ("groups", "dp"), "mp", "ctx"),
        P(None, ("groups", "dp"), "ctx"),
        P(("groups", "dp"), "ctx", None),
        P(None, "ctx", "mp"),
    )
    out_specs = (
        P(None, ("groups", "dp"), "ctx", "mp"),
        P(None, ("groups", "dp"), "ctx", None),
        P("groups", "ctx", "mp"),
    )
    return jax.shard_map(shards, mesh=mesh, in_specs=in_specs, out_specs=out_specs, check_vma=False)
```

profile of v0, /device:TPU:0, one launch (start us, length us, event | category | flops | bytes accessed | tf_op | source)
XLA Modules:
  0.0 406.5 jit_solution(13065868097995965039)
XLA Ops:
  8.7 5.4 %reduce-window.6 = f32[3,1,6,2,128]{4,3,2,1,0:T(2,128)S(1)} reduce-window(f32[3,1,6,2,128]{4,3,2,1,0:T(2,128)S(1)} %bitcast.295, f32[]{:T(128)} %constant.173.clone.1), window={size=1x1x1x1x128 pad=0_0x0_0x0_0x0_0x127_0}, to_apply=%region_0.0 | reduce-window | flops 585216 | bytes 36868 | tf_op jit(solution)/shard_map/reduce-window
  18.4 2.2 fusion.72
  23.2 14.1 %all-gather.1 = f32[12,1,6,1]{2,3,1,0:T(1,128)} all-gather(f32[3,1,6,1]{2,3,1,0:T(1,128)S(1)} %copy.107), channel_id=3, replica_groups=mesh['groups'=2,'ctx'=4,'dp'=2,'mp'=2] {'ctx'}, dimensions={0}, use_global_device_ids=true | all-gather | bytes 360 | tf_op jit(solution)/shard_map/all_gather | solution.py:14
  37.3 12.2 %all-gather.8.cloned.1.call-done = bf16[1,1024,768]{2,1,0:T(8,128)(2,1)} async-done(((bf16[1,256,768]{2,1,0:T(8,128)(2,1)}), bf16[1,1024,768]{2,1,0:T(8,128)(2,1)}) %all-gather.8.cloned.1.call-update) | async-done | bytes 1572880 | tf_op jit(solution)/shard_map/all_gather | solution.py:143
  49.6 3.6 gather_fusion
  53.2 2.9 gather_fusion.1
  56.1 45.0 %all-gather.14.cloned.1.call-done = f32[12,6,64,128]{3,2,1,0:T(8,128)} async-done(((f32[3,6,64,128]{3,2,1,0:T(8,128)}), f32[12,6,64,128]{3,2,1,0:T(8,128)}) %all-gather.14.cloned.1.call-update) | async-done | bytes 2359312 | tf_op jit(solution)/shard_map/all_gather | solution.py:14
  101.1 5.7 %while.69 = (s32[]{:T(128)}, f32[3,1,6,64,128]{4,3,2,1,0:T(8,128)S(1)}, s32[]{:T(128)}, f32[4,3,1,6]{3,2,1,0:T(1,128)}, f32[4,3,1,6,64,128]{5,4,3,1,2,0:T(8,128)}, /*index=5*/s32[]{:T(128)}, s32[]{:T(128)}) while((s32[]{:T(128)}, f32[3,1,6,64,128]{4,3,2,1,0:T(8,128)S(1)}, s32[]{:T(128)}, f32[4,3,1,6]{3,2,1,0:T(1,128)}, ...), condition=%wide.region_5.6_spmd.clone, body=%wide.region_4.5_spmd.clone.sunk | while | flops 589828 | bytes 1769937 | solution.py:26
  106.8 64.7 %all-gather.10.cloned.1.call-done = bf16[3,768,768]{2,1,0:T(8,128)(2,1)} async-done(((bf16[3,192,768]{2,1,0:T(8,128)(2,1)}), bf16[3,768,768]{2,1,0:T(8,128)(2,1)}) %all-gather.10.cloned.1.call-update) | async-done | bytes 3538960 | tf_op jit(solution)/shard_map/all_gather | solution.py:152
  171.5 3.3 fusion.71
  176.3 3.5 fusion.74
  180.2 27.0 %while.66 = (s32[]{:T(128)}, f32[3,1,6,64,128]{4,3,2,0,1:T(8,128)S(1)}, bf16[3,1,256,6,128]{2,4,3,0,1:T(8,128)(2,1)S(1)}, f32[2,3,1,6,64,128]{5,4,3,1,2,0:T(8,12...) while((s32[]{:T(128)}, ...), condition=%wide.region_8.9_spmd, body=%wide.region_6.8_spmd.sunk | while | flops 946094080 | bytes 10168943 | solution.py:99
  184.6 2.0 convolution_bitcast_fusion.8
  187.1 3.9 fusion.159
  191.2 2.5 fusion.157
  200.6 3.9 fusion.159
  204.6 2.5 fusion.157
  207.2 5.7 %fusion.82 = f32[3,768,768]{2,1,0:T(8,128)} fusion(bf16[3,256,768]{1,2,0:T(8,128)(2,1)S(1)} %bitcast.282, bf16[1,1,256,768]{3,2,0,1:T(8,128)(2,1)} %bitcast.290, bf16[1,1,256,768]{3,2,0,1:T(8,128)(2,1)S(1)} %bitcast.288, bf16[1,1,256,768]{3,2,0,1:T(8,128)(2,1)} %bitcast.292), kind=kOutput, calls=%fused_computation.120 | convolution fusion | flops 907149312 | bytes 9437184 | tf_op jit(solution)/shard_map/ovtd,ovti->odi/dot_general | solution.py:184
  216.0 13.1 %all-gather.12.cloned.1.call-done = f32[12,6,64,128]{3,2,1,0:T(8,128)} async-done(((f32[3,6,64,128]{3,2,1,0:T(8,128)}), f32[12,6,64,128]{3,2,1,0:T(8,128)}) %all-gather.12.cloned.1.call-update) | async-done | bytes 2359312 | tf_op jit(solution)/shard_map/all_gather | solution.py:14
  233.1 41.1 %while.67 = (s32[]{:T(128)}, f32[3,1,6,64,128]{4,3,2,0,1:T(8,128)S(1)}, bf16[3,1,256,6,128]{2,4,3,0,1:T(8,128)(2,1)S(1)}, f32[3,1,256,64]{2,3,0,1:T(8,128)}, f32...) while((s32[]{:T(128)}, ...), condition=%wide.region_12.13_spmd, body=%wide.region_9.12_spmd.sunk | while | flops 1929625600 | bytes 41488220 | solution.py:120
  241.0 2.3 fusion.182
  243.3 3.7 fusion.180
  247.5 2.6 fusion.179
  250.2 2.4 fusion.176
  255.7 2.0 convolution_bitcast_fusion.9
  261.5 2.3 fusion.182
  263.8 3.7 fusion.180
  268.0 2.7 fusion.179
  270.7 2.4 fusion.176
  278.0 5.0 %all-reduce.2 = bf16[3,1,256,128]{3,2,1,0:T(8,128)(2,1)} all-reduce(f32[3,1,256,128]{3,2,1,0:T(8,128)S(1)} %pad_maximum_fusion), channel_id=1, replica_groups=mesh['groups'=2,'ctx'=4,'dp'=2,'mp'=2] {'mp'}, use_global_device_ids=true, to_apply=%region_13.14 | all-reduce | flops 98304 | bytes 589824 | tf_op jit(solution)/shard_map/psum | solution.py:179
  283.0 70.6 %reduce-scatter.2.cloned.1.call-done = f32[3,192,768]{2,1,0:T(8,128)} async-done(((f32[3,768,768]{2,1,0:T(8,128)}), f32[3,192,768]{2,1,0:T(8,128)}) %reduce-scatter.2.cloned.1.call-update) | async-done | bytes 1769488 | tf_op jit(solution)/shard_map/reduce_scatter | solution.py:187
  353.6 46.3 %all-reduce.3 = bf16[3,192,768]{2,1,0:T(8,128)(2,1)} all-reduce(f32[3,192,768]{2,1,0:T(8,128)} %reduce-scatter.2.cloned.1.call-done), channel_id=1, replica_groups=mesh['groups'=2,'ctx'=4,'dp'=2,'mp'=2] {'dp'}, use_global_device_ids=true, to_apply=%region_15.16 | all-reduce | flops 442368 | bytes 2654208 | tf_op jit(solution)/shard_map/psum | solution.py:188
  (153 shorter events, 55.7 us)
Async XLA Ops:
  7.2 8.9 %copy-start.10 = (bf16[3,1,256,768]{3,2,1,0:T(8,128)(2,1)S(1)}, bf16[3,1,256,768]{3,2,1,0:T(8,128)(2,1)}, u32[]{:S(2)}) copy-start(bf16[3,1,256,768]{3,2,1,0:T(8,128)(2,1)} %param.14) | copy-start | bytes 3538948
  7.2 42.4 %all-gather.8.cloned.1.call-start = ((), (), s32[]{:S(2)}) async-start(), calls=%async_computation.1 | async-start | bytes 1966080 | tf_op jit(solution)/shard_map/all_gather | solution.py:143
  7.9 93.2 %all-gather.14.cloned.1.call-start = ((), (), s32[]{:S(2)}) async-start(), calls=%async_computation.5 | async-start | bytes 2949120 | tf_op jit(solution)/shard_map/all_gather | solution.py:14
  8.7 8.0 %copy-start.8 = (f32[3,1,6,256]{3,2,1,0:T(8,128)}, f32[3,1,6,256]{3,2,1,0:T(8,128)S(1)}, u32[]{:S(2)}) copy-start(f32[3,1,6,256]{3,2,1,0:T(8,128)S(1)} %fusion.84) | copy-start | bytes 55300
  20.6 150.9 %all-gather.10.cloned.1.call-start = ((), (), s32[]{:S(2)}) async-start(), calls=%async_computation.2 | async-start | bytes 4423680 | tf_op jit(solution)/shard_map/all_gather | solution.py:152
  21.3 207.8 %all-gather.12.cloned.1.call-start = ((), (), s32[]{:S(2)}) async-start(), calls=%async_computation.4 | async-start | bytes 2949120 | tf_op jit(solution)/shard_map/all_gather | solution.py:14
  21.5 15.8 %copy-start.14 = (s32[2,1,256]{2,1,0:T(1,128)S(1)}, s32[2,1,256]{2,1,0:T(1,128)}, u32[]{:S(2)}) copy-start(s32[2,1,256]{2,1,0:T(1,128)} %param.17) | copy-start | bytes 6148
  49.6 3.7 copy-start.1
  101.1 70.4 %copy-start.7 = (bf16[256,768]{1,0:T(8,128)(2,1)S(1)}, bf16[256,768]{1,0:T(8,128)(2,1)}, u32[]{:S(2)}) copy-start(bf16[256,768]{1,0:T(8,128)(2,1)} %gather_fusion) | copy-start | bytes 1179652
  174.8 1.5 copy-start.3
  179.8 173.8 %reduce-scatter.2.cloned.1.call-start = ((), (), s32[]{:S(2)}) async-start(), calls=%async_computation.3 | async-start | bytes 8847360 | tf_op jit(solution)/shard_map/reduce_scatter | solution.py:187
  207.2 5.8 %copy-start.2 = (f32[2,3,1,6,64,128]{5,4,3,1,2,0:T(8,128)}, f32[2,3,1,6,64,128]{5,4,3,1,2,0:T(8,128)S(1)}, u32[]{:S(2)}) copy-start(f32[2,3,1,6,64,128]{5,4,3,1,2,0:T(8,128)S(1)} %get-tuple-element.1132) | copy-start | bytes 3538948
  212.9 0.7 copy-start.13
  212.9 1.3 copy-start.4
  231.5 1.5 copy-start.9
  234.1 3.6 copy-start
  239.6 1.0 copy-start.5
  243.3 3.7 copy-start.11
  247.5 2.6 copy-start.12
  250.2 3.4 copy-start.6
  254.6 3.6 copy-start
  260.1 1.0 copy-start.5
  263.8 3.7 copy-start.11
  268.0 2.7 copy-start.12
  270.7 3.4 copy-start.6
Sparse Core Ops, SparseCore 0:
  9.6 39.9 all-gather.7
  51.7 49.3 all-gather.13
  102.7 68.7 all-gather.9
  180.0 49.1 all-gather.11
  231.3 122.3 reduce-scatter.1
where the time goes:
time: 408 us; the launch traced here: 406 us
  waiting for transfers between devices  207 us (51%)
  matrix products  66.1 us (16%)
  blocking collectives  65.4 us (16%)
  local copies, waits for them, and re-layouts  35.1 us (9%)
  other arithmetic  18 us (4%)
  between operations  14 us (3%)
    reduce_scatter x1, waiting for transfers between devices, shards(): lax.psum_scatter(weight_term, 'ctx', scatter_dimension=1, tiled=True)  70.6 us
    all_gather x1, waiting for transfers between devices, shards(): lax.all_gather(out_weight, 'ctx', axis=1, tiled=True)  64.7 us
    all_gather x2, waiting for transfers between devices, prefix(): pieces = jax.tree.map(lambda part: lax.all_gather(part, axis), value)  58.1 us
    dot_general x28, matrix products, contract(): return jnp.einsum(form, *operands, precision=EXACT)  57 us
    psum x1, blocking collectives, shards(): weight_grad = lax.psum(rows_sum, 'dp').astype(jnp.bfloat16)  46.3 us
    all_gather x1, blocking collectives, prefix(): pieces = jax.tree.map(lambda part: lax.all_gather(part, axis), value)  14.1 us
    all_gather x1, waiting for transfers between devices, shards(): gathered = lax.all_gather(cotangent, 'ctx', axis=1, tiled=True)  12.2 us
  transfers between devices with their start and end apart: 5, of which 5 were waited for; matrix products, arithmetic and copies ran while one was open for 26% of the time, Pallas kernels for 0%

commit v1 on v0

--- a/solution.py
+++ b/solution.py
@@ -7,6 +7,30 @@
 P_SIZE = 128
 N = 64
 EXACT = lax.Precision.HIGHEST
+
+
+def fill_patch(x_local, shard_axis, block_in):
+    newest = lax.psum(1, shard_axis)
+    all_rows = lax.axis_index(shard_axis)
+    then, r_now, known = (newest, all_rows, x_local.shape[1])
+    before = range(then)
+    formed = map(lambda k: (k, (k + 1) % then), before)
+    log = list(formed)
+    piece_out = range(then)
+    m_next = map(lambda k: (k, (k - 1) % then), piece_out)
+    sides = list(m_next)
+    latest = then // 2
+    far_arr = kept_arr = x_local
+    block_out = block_in(x_local, r_now * known)
+    for k0 in range(1, latest + 1):
+        far_arr = lax.ppermute(far_arr, shard_axis, log)
+        if k0 < then - latest:
+            kept_arr = lax.ppermute(kept_arr, shard_axis, sides)
+            ready = block_in(kept_arr, (r_now + k0) % then * known)
+            block_out = block_out + ready
+        inter = block_in(far_arr, (r_now - k0) % then * known)
+        block_out = block_out + inter
+    return block_out
 
 
 def prefix(value, axis, join, neutral, backward):
@@ -146,11 +170,15 @@
         return jax.vmap(lambda table_rows, row_ids: table_rows[row_ids])(gathered, ordering)
 
     scanned = jnp.stack([cotangent, reorder(scan_orders[0]), reorder(scan_orders[1])])
-    upstream = jnp.einsum(
-        "ovtd,odi->ovti",
-        scanned,
-        lax.all_gather(out_weight, "ctx", axis=1, tiled=True),
-        preferred_element_type=jnp.float32,
+    upstream = fill_patch(
+        out_weight,
+        "ctx",
+        lambda shard, at: jnp.einsum(
+            "ovtd,odi->ovti",
+            lax.dynamic_slice_in_dim(scanned, at, shard.shape[1], axis=3),
+            shard,
+            preferred_element_type=jnp.float32,
+        ),
     ).astype(jnp.bfloat16)
     upstream = lax.optimization_barrier(upstream)
     signal = head_inputs.astype(jnp.float32).reshape(3, volumes, tokens, local_heads, P_SIZE)

time: 408 us -> 383 us (0.939)
  waiting for transfers between devices: 207 us -> 116 us
  blocking collectives: 65.4 us -> 117 us
  starting transfers between devices: 0.38 us -> 5.57 us
  local copies, waits for them, and re-layouts: 35.1 us -> 39.5 us
    all_gather x1 -> x0, waiting for transfers between devices: 64.7 us -> none  [shards(): lax.all_gather(out_weight, 'ctx', axis=1, tiled=True)]
    all_gather x1, blocking collectives: 14.1 us -> 65.2 us  [prefix(): pieces = jax.tree.map(lambda part: lax.all_gather(part, axis), value)]
    all_gather x2, waiting for transfers between devices: 58.1 us -> 18.3 us  [prefix(): pieces = jax.tree.map(lambda part: lax.all_gather(part, axis), value)]
    ppermute x0 -> x3, waiting for transfers between devices: none -> 26.3 us  [the longest x2 26.3 us: fill_patch(): far_arr = lax.ppermute(far_arr, shard_axis, log)]
    all_gather x1, waiting for transfers between devices: 12.2 us -> 0.02 us  [shards(): gathered = lax.all_gather(cotangent, 'ctx', axis=1, tiled=True)]
    ppermute x0 -> x3, starting transfers between devices: none -> 5.23 us  [the longest x2 3.14 us: fill_patch(): far_arr = lax.ppermute(far_arr, shard_axis, log)]
    gather x3 -> x6, local copies, waits for them, and re-layouts: 6.56 us -> 9.64 us  [reorder(): table_rows[row_ids]]
  transfers between devices with their start and end apart: 5 -> 7, of which waited for: 5 -> 4; matrix products, arithmetic and copies ran while one was open for 26% -> 32% of each run, Pallas kernels for 0% -> 0%
where the time goes in v1:
time: 383 us; the launch traced here: 381 us
  blocking collectives  117 us (31%)
  waiting for transfers between devices  116 us (30%)
  matrix products  69.7 us (18%)
  local copies, waits for them, and re-layouts  39.5 us (10%)
  other arithmetic  19.4 us (5%)
  between operations  14 us (4%)
  starting transfers between devices  5.57 us (1%)
    reduce_scatter x1, waiting for transfers between devices, shards(): lax.psum_scatter(weight_term, 'ctx', scatter_dimension=1, tiled=True)  70.6 us
    all_gather x1, blocking collectives, prefix(): pieces = jax.tree.map(lambda part: lax.all_gather(part, axis), value)  65.2 us
    dot_general x28, matrix products, contract(): return jnp.einsum(form, *operands, precision=EXACT)  56.9 us
    psum x1, blocking collectives, shards(): weight_grad = lax.psum(rows_sum, 'dp').astype(jnp.bfloat16)  46.4 us
    ppermute x2, waiting for transfers between devices, fill_patch(): far_arr = lax.ppermute(far_arr, shard_axis, log)  26.3 us
    all_gather x2, waiting for transfers between devices, prefix(): pieces = jax.tree.map(lambda part: lax.all_gather(part, axis), value)  18.3 us
    gather x6, local copies, waits for them, and re-layouts, reorder(): table_rows[row_ids]  9.64 us
  transfers between devices with their start and end apart: 7, of which 4 were waited for; matrix products, arithmetic and copies ran while one was open for 32% of the time, Pallas kernels for 0%

profile of v1, /device:TPU:0, one launch (start us, length us, event | category | flops | bytes accessed | tf_op | source)
XLA Modules:
  0.0 381.4 jit_solution(9599549985815741837)
XLA Ops:
  8.7 5.4 %reduce-window.6 = f32[3,1,6,2,128]{4,3,2,1,0:T(2,128)S(1)} reduce-window(f32[3,1,6,2,128]{4,3,2,1,0:T(2,128)S(1)} %bitcast.309, f32[]{:T(128)} %constant.197.clone.1), window={size=1x1x1x1x128 pad=0_0x0_0x0_0x0_0x127_0}, to_apply=%region_0.1 | reduce-window | flops 585216 | bytes 36868 | tf_op jit(solution)/shard_map/reduce-window
  18.4 2.2 fusion.74
  20.6 3.1 collective-permute-start.1
  23.7 2.1 collective-permute-start
  28.6 65.2 %all-gather.1 = f32[12,1,6,1]{2,3,1,0:T(1,128)S(1)} all-gather(f32[3,1,6,1]{2,3,1,0:T(1,128)S(1)} %copy.116), channel_id=3, replica_groups=mesh['groups'=2,'ctx'=4,'dp'=2,'mp'=2] {'ctx'}, dimensions={0}, use_global_device_ids=true | all-gather | bytes 360 | tf_op jit(solution)/shard_map/all_gather | solution.py:38
  94.0 3.7 gather_fusion
  99.5 2.9 gather_fusion.1
  110.1 26.3 %collective-permute-done.2 = bf16[3,192,768]{2,1,0:T(8,128)(2,1)} collective-permute-done((bf16[3,192,768]{2,1,0:T(8,128)(2,1)}, bf16[3,192,768]{2,1,0:T(8,128)(2,1)}, u32[]{:S(2)}, u32[]{:S(2)}) %collective-permute-start.2) | collective-permute-done | bytes 884768 | tf_op jit(solution)/shard_map/ppermute | solution.py:26
  139.7 3.4 fusion.76
  143.4 5.0 %all-gather.11.cloned.1.call-done = f32[12,6,64,128]{3,2,1,0:T(8,128)} async-done(((f32[3,6,64,128]{3,2,1,0:T(8,128)}), f32[12,6,64,128]{3,2,1,0:T(8,128)}) %all-gather.11.cloned.1.call-update) | async-done | bytes 2359312 | tf_op jit(solution)/shard_map/all_gather | solution.py:38
  148.4 3.7 while.69
  153.3 28.9 %while.66 = (s32[]{:T(128)}, f32[3,1,6,64,128]{4,3,2,0,1:T(8,128)S(1)}, bf16[3,1,256,6,128]{2,4,3,0,1:T(8,128)(2,1)}, f32[2,3,1,6,64,128]{5,4,3,1,2,0:T(8,128)S(...) while((s32[]{:T(128)}, ...), condition=%wide.region_8.9_spmd, body=%wide.region_6.8_spmd.sunk | while | flops 946094080 | bytes 19606184 | solution.py:123
  157.7 2.0 convolution_bitcast_fusion.8
  160.3 4.0 %fusion.176 = bf16[3,1,256,6,128]{2,4,3,0,1:T(8,128)(2,1)S(1)} fusion(bf16[3,1,256,6,128]{2,4,3,0,1:T(8,128)(2,1)S(1)} %copy-done.3, s32[]{:T(128)S(6)} %select_n.245, f32[3,1,128,6,128]{2,4,3,0,1:T(8,128)S(1)} %convolution_bitcast_fusion.8, f32[3,1,256,6,128]{4,2,3,0,1:T(8,128)} %get-tuple-element.1115, f32[3,6,128]{2,1,0:T(8,128)S(1)} %bitcast.295, ...), kind=kOutput, calls=%fused_computation.15.clone.1 | convolution fusion | flops 454459392 | bytes 3777536 | tf_op jit(solution)/shard_map/while/body/eval_jaxpr/ovhij,ovjhp->ovihp/dot_general | solution.py:54
  165.3 2.5 fusion.174
  174.7 3.9 %fusion.176 = bf16[3,1,256,6,128]{2,4,3,0,1:T(8,128)(2,1)S(1)} fusion(bf16[3,1,256,6,128]{2,4,3,0,1:T(8,128)(2,1)S(1)} %copy-done.3, s32[]{:T(128)S(6)} %select_n.245, f32[3,1,128,6,128]{2,4,3,0,1:T(8,128)S(1)} %convolution_bitcast_fusion.8, f32[3,1,256,6,128]{4,2,3,0,1:T(8,128)} %get-tuple-element.1115, f32[3,6,128]{2,1,0:T(8,128)S(1)} %bitcast.295, ...), kind=kOutput, calls=%fused_computation.15.clone.1 | convolution fusion | flops 454459392 | bytes 3777536 | tf_op jit(solution)/shard_map/while/body/eval_jaxpr/ovhij,ovjhp->ovihp/dot_general | solution.py:54
  179.6 2.5 fusion.174
  182.2 6.0 %fusion.72 = f32[3,768,768]{2,1,0:T(8,128)} fusion(bf16[3,256,768]{1,2,0:T(8,128)(2,1)} %bitcast.296, bf16[1,1,256,768]{2,3,0,1:T(8,128)(2,1)} %bitcast.305, bf16[1,1,256,768]{2,3,0,1:T(8,128)(2,1)} %bitcast.303, bf16[1,1,256,768]{2,3,0,1:T(8,128)(2,1)S(1)} %bitcast.301), kind=kOutput, calls=%fused_computation.110 | convolution fusion | flops 907149312 | bytes 9437184 | tf_op jit(solution)/shard_map/ovtd,ovti->odi/dot_general | solution.py:212
  190.7 13.3 %all-gather.9.cloned.1.call-done = f32[12,6,64,128]{3,2,1,0:T(8,128)} async-done(((f32[3,6,64,128]{3,2,1,0:T(8,128)}), f32[12,6,64,128]{3,2,1,0:T(8,128)}) %all-gather.9.cloned.1.call-update) | async-done | bytes 2359312 | tf_op jit(solution)/shard_map/all_gather | solution.py:38
  207.9 41.1 %while.67 = (s32[]{:T(128)}, f32[3,1,6,64,128]{4,3,2,0,1:T(8,128)S(1)}, bf16[3,1,256,6,128]{2,4,3,0,1:T(8,128)(2,1)S(1)}, f32[3,1,256,64]{2,3,0,1:T(8,128)}, f32...) while((s32[]{:T(128)}, ...), condition=%wide.region_12.13_spmd, body=%wide.region_9.12_spmd.sunk | while | flops 1929625600 | bytes 41488220 | solution.py:144
  210.1 2.0 convolution_bitcast_fusion.9
  215.9 2.3 fusion.199
  218.2 3.7 fusion.197
  222.4 2.6 fusion.196
  225.1 2.4 fusion.193
  236.4 2.3 fusion.199
  238.7 3.7 fusion.197
  242.9 2.7 fusion.196
  245.6 2.4 fusion.193
  252.9 5.0 %all-reduce.2 = bf16[3,1,256,128]{3,2,1,0:T(8,128)(2,1)} all-reduce(f32[3,1,256,128]{3,2,1,0:T(8,128)S(1)} %pad_maximum_fusion.1), channel_id=1, replica_groups=mesh['groups'=2,'ctx'=4,'dp'=2,'mp'=2] {'mp'}, use_global_device_ids=true, to_apply=%region_13.14 | all-reduce | flops 98304 | bytes 589824 | tf_op jit(solution)/shard_map/psum | solution.py:207
  257.9 70.6 %reduce-scatter.2.cloned.1.call-done = f32[3,192,768]{2,1,0:T(8,128)} async-done(((f32[3,768,768]{2,1,0:T(8,128)}), f32[3,192,768]{2,1,0:T(8,128)}) %reduce-scatter.2.cloned.1.call-update) | async-done | bytes 1769488 | tf_op jit(solution)/shard_map/reduce_scatter | solution.py:215
  328.5 46.4 %all-reduce.3 = bf16[3,192,768]{2,1,0:T(8,128)(2,1)} all-reduce(f32[3,192,768]{2,1,0:T(8,128)} %reduce-scatter.2.cloned.1.call-done), channel_id=1, replica_groups=mesh['groups'=2,'ctx'=4,'dp'=2,'mp'=2] {'dp'}, use_global_device_ids=true, to_apply=%region_15.16 | all-reduce | flops 442368 | bytes 2654208 | tf_op jit(solution)/shard_map/psum | solution.py:216
  (177 shorter events, 67.8 us)
Async XLA Ops:
  7.2 8.9 %copy-start.12 = (bf16[3,1,256,768]{3,2,1,0:T(8,128)(2,1)S(1)}, bf16[3,1,256,768]{3,2,1,0:T(8,128)(2,1)}, u32[]{:S(2)}) copy-start(bf16[3,1,256,768]{3,2,1,0:T(8,128)(2,1)} %param.14) | copy-start | bytes 3538948
  7.2 86.8 %all-gather.7.cloned.1.call-start = ((), (), s32[]{:S(2)}) async-start(), calls=%async_computation.1 | async-start | bytes 1966080 | tf_op jit(solution)/shard_map/all_gather | solution.py:167
  7.9 140.5 %all-gather.11.cloned.1.call-start = ((), (), s32[]{:S(2)}) async-start(), calls=%async_computation.4 | async-start | bytes 2949120 | tf_op jit(solution)/shard_map/all_gather | solution.py:38
  8.7 8.0 %copy-start.10 = (f32[3,1,6,256]{3,2,1,0:T(8,128)}, f32[3,1,6,256]{3,2,1,0:T(8,128)S(1)}, u32[]{:S(2)}) copy-start(f32[3,1,6,256]{3,2,1,0:T(8,128)S(1)} %fusion.96) | copy-start | bytes 55300
  18.4 7.4 %copy-start.9 = (bf16[1,256,768]{2,1,0:T(8,128)(2,1)S(1)}, bf16[1,256,768]{2,1,0:T(8,128)(2,1)}, u32[]{:S(2)}) copy-start(bf16[1,256,768]{2,1,0:T(8,128)(2,1)} %param.18) | copy-start | bytes 1179652
  20.6 183.4 %all-gather.9.cloned.1.call-start = ((), (), s32[]{:S(2)}) async-start(), calls=%async_computation.3 | async-start | bytes 2949120 | tf_op jit(solution)/shard_map/all_gather | solution.py:38
  20.6 73.2 %collective-permute-start.1 = (bf16[3,192,768]{2,1,0:T(8,128)(2,1)}, bf16[3,192,768]{2,1,0:T(8,128)(2,1)}, u32[]{:S(2)}, u32[]{:S(2)}) collective-permute-start(bf16[3,192,768]{2,1,0:T(8,128)(2,1)} %param.19), channel_id=1, source_target_pairs={{0,4},{4,8},{8,12},{12,0},{1,5},{5,9},{9,13},{13,1},{2,6},{6,10},{... | collective-permute-start | bytes 2654216 | tf_op jit(solution)/shard_map/ppermute | solution.py:26
  23.7 84.7 %collective-permute-start = (bf16[3,192,768]{2,1,0:T(8,128)(2,1)}, bf16[3,192,768]{2,1,0:T(8,128)(2,1)}, u32[]{:S(2)}, u32[]{:S(2)}) collective-permute-start(bf16[3,192,768]{2,1,0:T(8,128)(2,1)} %param.19), channel_id=1, source_target_pairs={{0,12},{4,0},{8,4},{12,8},{1,13},{5,1},{9,5},{13,9},{2,14},{6,2},{... | collective-permute-start | bytes 2654216 | tf_op jit(solution)/shard_map/ppermute | solution.py:28
  26.8 67.0 %copy-start.19 = (s32[2,1,256]{2,1,0:T(1,128)S(1)}, s32[2,1,256]{2,1,0:T(1,128)}, u32[]{:S(2)}) copy-start(s32[2,1,256]{2,1,0:T(1,128)} %param.17) | copy-start | bytes 6148
  93.8 42.6 %collective-permute-start.2 = (bf16[3,192,768]{2,1,0:T(8,128)(2,1)}, bf16[3,192,768]{2,1,0:T(8,128)(2,1)}, u32[]{:S(2)}, u32[]{:S(2)}) collective-permute-start(bf16[3,192,768]{2,1,0:T(8,128)(2,1)} %collective-permute-done.1), channel_id=1, source_target_pairs={{0,4},{4,8},{8,12},{12,0},{1,5},{5,9},{9,13},{13,1},{2,6},{6,10},{... | collective-permute-start | bytes 2654216 | tf_op jit(solution)/shard_map/ppermute | solution.py:26
  93.9 5.6 %copy-start.1 = (bf16[1,1024,768]{2,1,0:T(8,128)(2,1)S(1)}, bf16[1,1024,768]{2,1,0:T(8,128)(2,1)}, u32[]{:S(2)}) copy-start(bf16[1,1024,768]{2,1,0:T(8,128)(2,1)} %all-gather.7.cloned.1.call-done) | copy-start | bytes 4718596
  103.6 1.4 copy-start.8
  138.3 1.5 copy-start.15
  138.3 1.5 copy-start.16
  143.2 185.3 %reduce-scatter.2.cloned.1.call-start = ((), (), s32[]{:S(2)}) async-start(), calls=%async_computation.2 | async-start | bytes 8847360 | tf_op jit(solution)/shard_map/reduce_scatter | solution.py:215
  152.1 1.1 copy-start.17
  153.2 28.9 %copy-start.7 = (bf16[1,256,768]{1,2,0:T(8,128)(2,1)S(1)}, bf16[1,256,768]{1,2,0:T(8,128)(2,1)}, u32[]{:S(2)}) copy-start(bf16[1,256,768]{1,2,0:T(8,128)(2,1)} %copy.110) | copy-start | bytes 1179652
  157.7 2.6 copy-start.3
  164.2 1.0 copy-start.4
  172.2 2.6 copy-start.3
  178.6 1.0 copy-start.4
  182.2 6.0 %copy-start.2 = (f32[2,3,1,6,64,128]{5,4,3,1,2,0:T(8,128)}, f32[2,3,1,6,64,128]{5,4,3,1,2,0:T(8,128)S(1)}, u32[]{:S(2)}) copy-start(f32[2,3,1,6,64,128]{5,4,3,1,2,0:T(8,128)S(1)} %get-tuple-element.1132) | copy-start | bytes 3538948
  206.4 1.5 copy-start.11
  209.0 3.6 copy-start
  218.2 3.7 copy-start.13
  222.4 2.6 copy-start.14
  225.1 3.4 copy-start.6
  229.5 3.6 copy-start
  235.0 1.0 copy-start.5
  238.7 3.7 copy-start.13
  242.9 2.7 copy-start.14
  245.6 3.4 copy-start.6
  (2 other events, 1.7 us)
Sparse Core Ops, SparseCore 0:
  9.6 69.8 all-gather.6
  81.0 67.2 all-gather.10
  150.5 53.4 all-gather.8
  206.2 122.3 reduce-scatter.1
